TPU v7x, 32 devices: a whole 2x2x4 slice. The times are simulated.
32 devices in a mesh: group: 2 (over x), cell: 16 (over z, y, core).
Axes of the slice: x: 2, y: 2, z: 4, core: 2. Of those that a mesh axis runs over, the one named last changes fastest.
Arguments:
- adjoint_seed: float32 [32, 5, 16384], P('group', None, 'cell'), parts along dimension 0, may hold values from -6 to 6
- inv_blocks: bfloat16 [32, 5, 5, 16384], P('group', None, None, 'cell'), parts along dimension 0
- flux_jacobians: float32 [2, 32, 5, 5], P(None, 'group'), parts along dimension 1, may hold values from -1.5 to 1.5
- modal_shapes: float32 [20, 5, 16384], P(None, None, 'cell'), may hold values from -0.01953125 to 0.01953125
- modal_gain: float32 [40], P('group'), parts along dimension 0, may hold values from 0.05 to 0.3
- face_cells: int32 [2, 49152], P(None, 'cell'), may hold values from 0 to 1279, as said below
- face_weights: float32 [49152], P('cell'), may hold values from 0.4 to 1
- colours: int32 [16384], P('cell'), may hold values from 0 to 1
- send_cells: int32 [2, 2048], P(None, 'cell'), may hold values from 0 to 1023, as said below
Outputs:
- adjoint_state: float32 [32, 5, 16384], P('group', None, 'cell'), parts along dimension 0
- modal_partials: float32 [32, 20], P('group'), parts along dimension 0
There are 2 independent parts, one for each index of `group`. A program takes and returns all parts, laid end to end along the dimension named above; an argument that names none is the same for every part. Nothing has to cross between parts.
Inputs may be any that keep to these rules, and one draw needn't show every extreme that they name: `face_cells`: each face's left cell is a local cell or a lower ghost (from 1024 to 1151); its right cell is a local cell or an upper ghost (from 1152 on). `send_cells`: within a partition the 256 listed cells are distinct local cells.
All inputs are finite; a program needn't handle non-finite values.
Results may differ from a plain program's by a relative error of at most 0.0003.
Values sent between devices are 32-bit elements; how exact they have to be, the bound alone decides.
A program may use at most 64 MiB of HBM per device.

v0:
```python
import math

import jax
import jax.numpy as jnp
import numpy as np
from jax import lax
from jax.sharding import PartitionSpec as P

ITERS = 4


frequency = 0.04


def from_behind(value, axis, by):
    devices = lax.axis_size(axis)
    return lax.ppermute(value, axis, [(i, (i + by) % devices) for i in range(devices)])


def spectral_matrix(count):
    index = jnp.arange(count)
    apart = index[:, None] - index[None, :]
    angle = math.pi * apart.astype(jnp.float32) / count
    parity = jnp.where(apart % 2 == 0, 1.0, -1.0).astype(jnp.float32)
    safe_sin = jnp.where(apart == 0, 1.0, jnp.sin(angle))
    return jnp.where(apart == 0, 0.0, 0.5 * parity * jnp.cos(angle) / safe_sin)


def wide_dot(left, right):
    return jnp.dot(left, right, precision=lax.Precision.HIGHEST, preferred_element_type=jnp.float32)


def modal_total(state_rows, shape_rows, count, nvar, modes):
    gram = lax.dot_general(
        state_rows,
        shape_rows,
        (((1,), (1,)), ((), ())),
        precision=lax.Precision.HIGHEST,
        preferred_element_type=jnp.float32,
    )
    local_part = jnp.einsum("ivmv->im", gram.reshape(count, nvar, modes, nvar))
    return lax.psum(local_part, "cell")


def local(
    adjoint_seed,
    inv_blocks,
    flux_jacobians,
    modal_shapes,
    modal_gain,
    face_cells,
    face_weights,
    colours,
    send_cells,
):
    count, nvar, owned = adjoint_seed.shape
    modes = modal_shapes.shape[0]
    rows = count * nvar
    eye_inst = jnp.eye(count, dtype=jnp.float32)
    eye_var = jnp.eye(nvar, dtype=jnp.float32)
    left_matrix = jnp.einsum("ij,ivw->iwjv", eye_inst, flux_jacobians[0]).reshape(rows, rows)
    right_matrix = jnp.einsum("ij,ivw->iwjv", eye_inst, flux_jacobians[1]).reshape(rows, rows)
    spectral = spectral_matrix(count)
    spectral_rows = frequency * jnp.einsum("jk,vu->kvju", spectral, eye_var).reshape(rows, rows)
    seed_rows = adjoint_seed.reshape(rows, owned)
    shape_rows = modal_shapes.reshape(modes * nvar, owned)
    flat_inverse = inv_blocks.reshape(count * nvar * nvar, owned)
    inst_index = np.arange(count)[:, None]
    out_index = np.arange(nvar)[None, :]
    inverse_parts = []
    source_rows = []
    for var in range(nvar):
        pick = (inst_index * nvar * nvar + var * nvar + out_index).reshape(-1)
        inverse_parts.append(
            jnp.take(flat_inverse, jnp.asarray(pick, jnp.int32), axis=0).astype(jnp.float32)
        )
        source_rows.append(
            jnp.asarray((inst_index * nvar + var + 0 * out_index).reshape(-1), jnp.int32)
        )
    left_cells = face_cells[0]
    right_cells = face_cells[1]
    colour_mask = colours[None, :]
    state = jnp.zeros_like(seed_rows)
    for sweep in range(ITERS):
        lam = modal_total(state, shape_rows, count, nvar, modes) * modal_gain[None, :]
        lift = jnp.einsum("im,vu->ivmu", lam, eye_var).reshape(rows, modes * nvar)
        base = seed_rows + wide_dot(lift, shape_rows)
        to_lower = jnp.take(state, send_cells[0], axis=1)
        to_upper = jnp.take(state, send_cells[1], axis=1)
        from_lower = from_behind(to_upper, "cell", 1)
        from_upper = from_behind(to_lower, "cell", -1)
        ghosts = jnp.concatenate([from_lower, from_upper], axis=1)
        for colour in range(2):
            extended = jnp.concatenate([state, ghosts], axis=1)
            from_left = wide_dot(left_matrix, extended)
            from_right = wide_dot(right_matrix, extended)
            total = jnp.zeros_like(extended)
            total = total.at[:, right_cells].add(
                face_weights * jnp.take(from_left, left_cells, axis=1)
            )
            total = total.at[:, left_cells].add(
                face_weights * jnp.take(from_right, right_cells, axis=1)
            )
            spectral_term = wide_dot(spectral_rows, state)
            resid = base - total[:, :owned] - spectral_term
            updated = inverse_parts[0] * jnp.take(resid, source_rows[0], axis=0)
            for var in range(1, nvar):
                updated = updated + inverse_parts[var] * jnp.take(resid, source_rows[var], axis=0)
            state = jnp.where(colour_mask == colour, updated, state)
    partials = modal_total(state, shape_rows, count, nvar, modes)
    return (state.reshape(count, nvar, owned), partials)


def solution(mesh):
    return jax.shard_map(
        local,
        mesh=mesh,
        in_specs=(
            P("group", None, "cell"),
            P("group", None, None, "cell"),
            P(None, "group", None, None),
            P(None, None, "cell"),
            P("group"),
            P(None, "cell"),
            P("cell"),
            P("cell"),
            P(None, "cell"),
        ),
        out_specs=(P("group", None, "cell"), P("group", None)),
        check_vma=False,
    )
```

profile of v0, /device:TPU:0, one launch (start us, length us, event | category | flops | bytes accessed | tf_op | source)
XLA Modules:
  0.0 821.1 jit_solution(13111969591882598238)
XLA Ops:
  2.9 5.4 collective-permute-start.1
  12.7 34.5 %psum.35 = f32[16,20]{1,0:T(8,128)S(1)} all-reduce(f32[16,20]{1,0:T(8,128)S(1)} %fusion.48), channel_id=1, replica_groups=mesh['group'=2,'cell'=16] {'cell'}, use_global_device_ids=true, to_apply=%region_1.3 | all-reduce | flops 320 | bytes 2560 | tf_op jit(solution)/shard_map/psum | solution.py:42
  65.2 26.8 %scatter_custom_fusion = f32[80,1280]{0,1:T(8,128)} fusion(s32[3072]{0:T(1024)} %bitcast.273, f32[]{:T(128)} %constant.24.clone.8, f32[3072]{0:T(1024)S(1)} %copy-done.1, pred[3072]{0:T(1024)(128)(4,1)S(1)} %compare_and_fusion, f32[]{:T(128)} %constant.44.clone.1, f32[80,1280]{0,1:T(8,128)S(1)} %fusion.107, s32[3072]{0:T(1024)S(1)} %fusion.178), kind=kCustom, calls=%fused_computation.130 | custom fusion | flops 737280 | bytes 847872 | tf_op jit(solution)/shard_map/scatter-add | solution.py:98
  94.0 27.7 %scatter_custom_fusion.1 = f32[80,1280]{0,1:T(8,128)} fusion(f32[80,1280]{0,1:T(8,128)} %scatter_custom_fusion, s32[3072]{0:T(1024)} %bitcast.265, f32[]{:T(128)} %constant.24.clone.8, f32[3072]{0:T(1024)S(1)} %copy-done.1, pred[3072]{0:T(1024)(128)(4,1)S(1)} %compare_and_fusion.1, f32[80,1280]{0,1:T(8,128)S(1)} %fusion.106, s32[3072]{0:T(1024)S(1)} %fusion.177), kind=kCustom, calls=%fused_computation.127 | custom fusion | flops 737280 | bytes 847360 | tf_op jit(solution)/shard_map/scatter-add | solution.py:101
  132.2 27.0 %scatter_custom_fusion.2 = f32[80,1280]{0,1:T(8,128)} fusion(s32[3072]{0:T(1024)} %bitcast.274, f32[]{:T(128)} %constant.24.clone.8, f32[3072]{0:T(1024)S(1)} %copy-done.1, pred[3072]{0:T(1024)(128)(4,1)S(1)} %compare_and_fusion, f32[]{:T(128)} %constant.44.clone.1, f32[80,1280]{0,1:T(8,128)S(1)} %fusion.174, s32[3072]{0:T(1024)S(1)} %fusion.178), kind=kCustom, calls=%fused_computation.124 | custom fusion | flops 737280 | bytes 847872 | tf_op jit(solution)/shard_map/scatter-add | solution.py:98
  161.2 27.7 %scatter_custom_fusion.3 = f32[80,1280]{0,1:T(8,128)} fusion(f32[80,1280]{0,1:T(8,128)} %scatter_custom_fusion.2, s32[3072]{0:T(1024)} %bitcast.266, f32[]{:T(128)} %constant.24.clone.8, f32[3072]{0:T(1024)S(1)} %copy-done.1, pred[3072]{0:T(1024)(128)(4,1)S(1)} %compare_and_fusion.1, f32[80,1280]{0,1:T(8,128)S(1)} %fusion.173, s32[3072]{0:T(1024)S(1)} %fusion.177), kind=kCustom, calls=%fused_computation.121 | custom fusion | flops 737280 | bytes 847360 | tf_op jit(solution)/shard_map/scatter-add | solution.py:101
  204.1 2.6 fusion.49
  206.7 30.0 %psum.36 = f32[16,20]{1,0:T(8,128)S(1)} all-reduce(f32[16,20]{1,0:T(8,128)S(1)} %fusion.49), channel_id=1, replica_groups=mesh['group'=2,'cell'=16] {'cell'}, use_global_device_ids=true, to_apply=%region_7.12 | all-reduce | flops 320 | bytes 2560 | tf_op jit(solution)/shard_map/psum | solution.py:42
  241.2 4.2 collective-permute-done.2
  247.9 26.6 %scatter_custom_fusion.4 = f32[80,1280]{0,1:T(8,128)} fusion(s32[3072]{0:T(1024)} %bitcast.275, f32[]{:T(128)} %constant.24.clone.8, f32[3072]{0:T(1024)S(1)} %copy-done.1, pred[3072]{0:T(1024)(128)(4,1)S(1)} %compare_and_fusion, f32[]{:T(128)} %constant.44.clone.1, f32[80,1280]{0,1:T(8,128)S(1)} %fusion.170, s32[3072]{0:T(1024)S(1)} %fusion.178), kind=kCustom, calls=%fused_computation.118 | custom fusion | flops 737280 | bytes 847872 | tf_op jit(solution)/shard_map/scatter-add | solution.py:98
  276.6 27.9 %scatter_custom_fusion.5 = f32[80,1280]{0,1:T(8,128)} fusion(f32[80,1280]{0,1:T(8,128)} %scatter_custom_fusion.4, s32[3072]{0:T(1024)} %bitcast.267, f32[]{:T(128)} %constant.24.clone.8, f32[3072]{0:T(1024)S(1)} %copy-done.1, pred[3072]{0:T(1024)(128)(4,1)S(1)} %compare_and_fusion.1, f32[80,1280]{0,1:T(8,128)S(1)} %fusion.169, s32[3072]{0:T(1024)S(1)} %fusion.177), kind=kCustom, calls=%fused_computation.115 | custom fusion | flops 737280 | bytes 847360 | tf_op jit(solution)/shard_map/scatter-add | solution.py:101
  316.5 2.1 fusion.172
  318.5 37.3 %scatter_custom_fusion.6 = f32[80,1280]{0,1:T(8,128)} fusion(s32[3072]{0:T(1024)} %bitcast.276, f32[]{:T(128)} %constant.24.clone.8, f32[3072]{0:T(1024)S(1)} %copy-done.1, pred[3072]{0:T(1024)(128)(4,1)S(1)} %compare_and_fusion, f32[]{:T(128)} %constant.44.clone.1, f32[80,1280]{0,1:T(8,128)} %fusion.172, s32[3072]{0:T(1024)S(1)} %fusion.178), kind=kCustom, calls=%fused_computation.112 | custom fusion | flops 737280 | bytes 1093632 | tf_op jit(solution)/shard_map/scatter-add | solution.py:98
  355.9 2.1 fusion.171
  357.9 38.8 %scatter_custom_fusion.7 = f32[80,1280]{0,1:T(8,128)} fusion(f32[80,1280]{0,1:T(8,128)} %scatter_custom_fusion.6, s32[3072]{0:T(1024)} %bitcast.268, f32[]{:T(128)} %constant.24.clone.8, f32[3072]{0:T(1024)S(1)} %copy-done.1, pred[3072]{0:T(1024)(128)(4,1)S(1)} %compare_and_fusion.1, f32[80,1280]{0,1:T(8,128)} %fusion.171, s32[3072]{0:T(1024)S(1)} %fusion.177), kind=kCustom, calls=%fused_computation.109 | custom fusion | flops 737280 | bytes 1093120 | tf_op jit(solution)/shard_map/scatter-add | solution.py:101
  411.2 2.6 fusion.50
  413.8 30.2 %psum.37 = f32[16,20]{1,0:T(8,128)S(1)} all-reduce(f32[16,20]{1,0:T(8,128)S(1)} %fusion.50), channel_id=1, replica_groups=mesh['group'=2,'cell'=16] {'cell'}, use_global_device_ids=true, to_apply=%region_13.18 | all-reduce | flops 320 | bytes 2560 | tf_op jit(solution)/shard_map/psum | solution.py:42
  448.5 4.0 collective-permute-done.4
  455.1 26.8 %scatter_custom_fusion.8 = f32[80,1280]{0,1:T(8,128)} fusion(s32[3072]{0:T(1024)} %bitcast.277, f32[]{:T(128)} %constant.24.clone.8, f32[3072]{0:T(1024)S(1)} %copy-done.1, pred[3072]{0:T(1024)(128)(4,1)S(1)} %compare_and_fusion, f32[]{:T(128)} %constant.44.clone.1, f32[80,1280]{0,1:T(8,128)S(1)} %fusion.166, s32[3072]{0:T(1024)S(1)} %fusion.178), kind=kCustom, calls=%fused_computation.106 | custom fusion | flops 737280 | bytes 847872 | tf_op jit(solution)/shard_map/scatter-add | solution.py:98
  483.9 27.7 %scatter_custom_fusion.9 = f32[80,1280]{0,1:T(8,128)} fusion(f32[80,1280]{0,1:T(8,128)} %scatter_custom_fusion.8, s32[3072]{0:T(1024)} %bitcast.269, f32[]{:T(128)} %constant.24.clone.8, f32[3072]{0:T(1024)S(1)} %copy-done.1, pred[3072]{0:T(1024)(128)(4,1)S(1)} %compare_and_fusion.1, f32[80,1280]{0,1:T(8,128)S(1)} %fusion.165, s32[3072]{0:T(1024)S(1)} %fusion.177), kind=kCustom, calls=%fused_computation.103 | custom fusion | flops 737280 | bytes 847360 | tf_op jit(solution)/shard_map/scatter-add | solution.py:101
  523.6 2.1 fusion.168
  525.6 37.5 %scatter_custom_fusion.10 = f32[80,1280]{0,1:T(8,128)} fusion(s32[3072]{0:T(1024)} %bitcast.278, f32[]{:T(128)} %constant.24.clone.8, f32[3072]{0:T(1024)S(1)} %copy-done.1, pred[3072]{0:T(1024)(128)(4,1)S(1)} %compare_and_fusion, f32[]{:T(128)} %constant.44.clone.1, f32[80,1280]{0,1:T(8,128)} %fusion.168, s32[3072]{0:T(1024)S(1)} %fusion.178), kind=kCustom, calls=%fused_computation.100 | custom fusion | flops 737280 | bytes 1093632 | tf_op jit(solution)/shard_map/scatter-add | solution.py:98
  563.2 2.1 fusion.167
  565.3 38.4 %scatter_custom_fusion.11 = f32[80,1280]{0,1:T(8,128)} fusion(f32[80,1280]{0,1:T(8,128)} %scatter_custom_fusion.10, s32[3072]{0:T(1024)} %bitcast.270, f32[]{:T(128)} %constant.24.clone.8, f32[3072]{0:T(1024)S(1)} %copy-done.1, pred[3072]{0:T(1024)(128)(4,1)S(1)} %compare_and_fusion.1, f32[80,1280]{0,1:T(8,128)} %fusion.167, s32[3072]{0:T(1024)S(1)} %fusion.177), kind=kCustom, calls=%fused_computation.97 | custom fusion | flops 737280 | bytes 1093120 | tf_op jit(solution)/shard_map/scatter-add | solution.py:101
  618.1 2.6 fusion.51
  620.7 30.4 %psum.38 = f32[16,20]{1,0:T(8,128)S(1)} all-reduce(f32[16,20]{1,0:T(8,128)S(1)} %fusion.51), channel_id=1, replica_groups=mesh['group'=2,'cell'=16] {'cell'}, use_global_device_ids=true, to_apply=%region_19.24 | all-reduce | flops 320 | bytes 2560 | tf_op jit(solution)/shard_map/psum | solution.py:42
  655.0 5.0 collective-permute-done.6
  661.8 26.0 %scatter_custom_fusion.12 = f32[80,1280]{0,1:T(8,128)S(1)} fusion(s32[3072]{0:T(1024)} %bitcast.279, f32[]{:T(128)} %constant.24.clone.8, f32[3072]{0:T(1024)S(1)} %copy-done.1, pred[3072]{0:T(1024)(128)(4,1)S(1)} %compare_and_fusion, f32[]{:T(128)} %constant.44.clone.1, f32[80,1280]{0,1:T(8,128)S(1)} %fusion.162, s32[3072]{0:T(1024)S(1)} %fusion.178), kind=kCustom, calls=%fused_computation.94 | custom fusion | flops 737280 | bytes 847872 | tf_op jit(solution)/shard_map/scatter-add | solution.py:98
  689.0 26.2 %scatter_custom_fusion.13 = f32[80,1280]{0,1:T(8,128)S(1)} fusion(f32[80,1280]{0,1:T(8,128)S(1)} %scatter_custom_fusion.12, s32[3072]{0:T(1024)} %bitcast.271, f32[]{:T(128)} %constant.24.clone.8, f32[3072]{0:T(1024)S(1)} %copy-done.1, pred[3072]{0:T(1024)(128)(4,1)S(1)} %compare_and_fusion.1, f32[80,1280]{0,1:T(8,128)S(1)} %fusion.161, s32[3072]{0:T(1024)S(1)} %fusion.177), kind=kCustom, calls=%fused_computation.91 | custom fusion | flops 737280 | bytes 1093120 | tf_op jit(solution)/shard_map/scatter-add | solution.py:101
  724.1 26.6 %scatter_custom_fusion.14 = f32[80,1280]{0,1:T(8,128)} fusion(s32[3072]{0:T(1024)} %bitcast.280, f32[]{:T(128)} %constant.24.clone.8, f32[3072]{0:T(1024)S(1)} %copy-done.1, pred[3072]{0:T(1024)(128)(4,1)S(1)} %compare_and_fusion, f32[]{:T(128)} %constant.44.clone.1, f32[80,1280]{0,1:T(8,128)S(1)} %fusion.164, s32[3072]{0:T(1024)S(1)} %fusion.178), kind=kCustom, calls=%fused_computation.88 | custom fusion | flops 737280 | bytes 847872 | tf_op jit(solution)/shard_map/scatter-add | solution.py:98
  751.9 27.9 %scatter_custom_fusion.15 = f32[80,1280]{0,1:T(8,128)} fusion(f32[80,1280]{0,1:T(8,128)} %scatter_custom_fusion.14, s32[3072]{0:T(1024)} %bitcast.272, f32[]{:T(128)} %constant.24.clone.8, f32[3072]{0:T(1024)S(1)} %copy-done.1, pred[3072]{0:T(1024)(128)(4,1)S(1)} %compare_and_fusion.1, f32[80,1280]{0,1:T(8,128)S(1)} %fusion.163, s32[3072]{0:T(1024)S(1)} %fusion.177), kind=kCustom, calls=%fused_computation.85 | custom fusion | flops 737280 | bytes 847360 | tf_op jit(solution)/shard_map/scatter-add | solution.py:101
  790.2 30.6 %psum.39 = f32[16,20]{1,0:T(8,128)} all-reduce(f32[16,20]{1,0:T(8,128)S(1)} %fusion.52), channel_id=1, replica_groups=mesh['group'=2,'cell'=16] {'cell'}, use_global_device_ids=true, to_apply=%region_25.30 | all-reduce | flops 320 | bytes 2560 | tf_op jit(solution)/shard_map/psum | solution.py:42
  (302 shorter events, 151.8 us)
Async XLA Ops:
  0.6 9.1 %copy-start.24 = (s32[2,3072]{1,0:T(2,128)S(1)}, s32[2,3072]{1,0:T(2,128)}, u32[]{:S(2)}) copy-start(s32[2,3072]{1,0:T(2,128)} %param.32) | copy-start | bytes 73732
  0.6 10.0 %copy-start.23 = (f32[16,5,1024]{2,0,1:T(8,128)S(1)}, f32[16,5,1024]{2,0,1:T(8,128)}, u32[]{:S(2)}) copy-start(f32[16,5,1024]{2,0,1:T(8,128)} %param.27) | copy-start | bytes 983044
  1.4 7.6 copy-start.31
  1.4 7.6 copy-start.35
  1.4 7.6 copy-start.36
  2.2 8.7 %copy-start = (f32[20,5,1024]{2,0,1:T(8,128)S(1)}, f32[20,5,1024]{2,0,1:T(8,128)}, u32[]{:S(2)}) copy-start(f32[20,5,1024]{2,0,1:T(8,128)} %param.30) | copy-start | bytes 1228804
  2.9 59.0 %collective-permute-start.1 = (f32[80,128]{1,0:T(8,128)}, f32[80,128]{1,0:T(8,128)S(1)}, u32[]{:S(2)}, u32[]{:S(2)}) collective-permute-start(f32[80,128]{1,0:T(8,128)} %select_bitcast_fusion.6), channel_id=1, source_target_pairs={{0,15},{1,0},{2,1},{3,2},{4,3},{5,4},{6,5},{7,6},{8,7},{9,8},{10,9... | collective-permute-start | bytes 122888 | tf_op jit(solution)/shard_map/ppermute | solution.py:17
  9.7 52.2 %collective-permute-start = (f32[80,128]{1,0:T(8,128)}, f32[80,128]{1,0:T(8,128)S(1)}, u32[]{:S(2)}, u32[]{:S(2)}) collective-permute-start(f32[80,128]{1,0:T(8,128)} %select_bitcast_fusion.7), channel_id=1, source_target_pairs={{0,1},{1,2},{2,3},{3,4},{4,5},{5,6},{6,7},{7,8},{8,9},{9,10},{10,1... | collective-permute-start | bytes 122888 | tf_op jit(solution)/shard_map/ppermute | solution.py:17
  10.8 36.4 %copy-start.38 = (f32[20]{0:T(128)S(1)}, f32[20]{0:T(128)}, u32[]{:S(2)}) copy-start(f32[20]{0:T(128)} %param.31) | copy-start | bytes 244
  47.4 3.4 copy-start.45
  47.4 3.4 copy-start.44
  47.6 3.9 copy-start.42
  61.1 4.0 copy-start.1
  201.7 35.0 %copy-start.39 = (f32[20]{0:T(128)S(1)}, f32[20]{0:T(128)}, u32[]{:S(2)}) copy-start(f32[20]{0:T(128)} %param.31) | copy-start | bytes 244
  204.1 34.9 %copy-start.32 = (pred[128]{0:T(512)(128)(4,1)S(1)}, pred[128]{0:T(512)(128)(4,1)}, u32[]{:S(2)}) copy-start(pred[128]{0:T(512)(128)(4,1)} %copy-done.31) | copy-start | bytes 388
  238.9 1.7 collective-permute-start.3
  239.0 6.3 collective-permute-start.2
  316.5 39.4 %copy-start.13 = (f32[80,128]{1,0:T(8,128)S(1)}, f32[80,128]{1,0:T(8,128)}, u32[]{:S(2)}) copy-start(f32[80,128]{1,0:T(8,128)} %copy-done.11) | copy-start | bytes 122884
  316.5 39.4 %copy-start.19 = (f32[80,128]{1,0:T(8,128)S(1)}, f32[80,128]{1,0:T(8,128)}, u32[]{:S(2)}) copy-start(f32[80,128]{1,0:T(8,128)} %copy-done.17) | copy-start | bytes 122884
  408.8 35.2 %copy-start.40 = (f32[20]{0:T(128)S(1)}, f32[20]{0:T(128)}, u32[]{:S(2)}) copy-start(f32[20]{0:T(128)} %param.31) | copy-start | bytes 244
  411.2 35.1 %copy-start.33 = (pred[128]{0:T(512)(128)(4,1)S(1)}, pred[128]{0:T(512)(128)(4,1)}, u32[]{:S(2)}) copy-start(pred[128]{0:T(512)(128)(4,1)} %copy-done.31) | copy-start | bytes 388
  446.2 1.7 collective-permute-start.5
  446.3 6.2 collective-permute-start.4
  523.6 39.6 %copy-start.16 = (f32[80,128]{1,0:T(8,128)S(1)}, f32[80,128]{1,0:T(8,128)}, u32[]{:S(2)}) copy-start(f32[80,128]{1,0:T(8,128)} %copy-done.14) | copy-start | bytes 122884
  523.6 39.6 %copy-start.22 = (f32[80,128]{1,0:T(8,128)S(1)}, f32[80,128]{1,0:T(8,128)}, u32[]{:S(2)}) copy-start(f32[80,128]{1,0:T(8,128)} %copy-done.20) | copy-start | bytes 122884
  615.8 35.3 %copy-start.41 = (f32[20]{0:T(128)S(1)}, f32[20]{0:T(128)}, u32[]{:S(2)}) copy-start(f32[20]{0:T(128)} %param.31) | copy-start | bytes 244
  618.1 35.3 %copy-start.34 = (pred[128]{0:T(512)(128)(4,1)S(1)}, pred[128]{0:T(512)(128)(4,1)}, u32[]{:S(2)}) copy-start(pred[128]{0:T(512)(128)(4,1)} %copy-done.31) | copy-start | bytes 388
  653.3 1.7 collective-permute-start.7
  653.4 6.6 collective-permute-start.6
  655.0 5.0 copy-start.7
  661.8 26.0 %copy-start.8 = (f32[80,128]{1,0:T(8,128)S(1)}, f32[80,128]{1,0:T(8,128)}, u32[]{:S(2)}) copy-start(f32[80,128]{1,0:T(8,128)} %copy-done.7) | copy-start | bytes 122884
  661.8 26.0 %copy-start.10 = (f32[80,128]{1,0:T(8,128)S(1)}, f32[80,128]{1,0:T(8,128)}, u32[]{:S(2)}) copy-start(f32[80,128]{1,0:T(8,128)} %copy-done.9) | copy-start | bytes 122884
  (29 other events, 44.6 us)
where the time goes:
time: 833 us; the launch traced here: 821 us
  other arithmetic  498 us (60%)
  blocking collectives  156 us (19%)
  local copies, waits for them, and re-layouts  96.2 us (12%)
  matrix products  47.3 us (6%)
  waiting for transfers between devices  14.2 us (2%)
    scatter-add x8, other arithmetic, local(): total.at[:, left_cells]  242 us
    scatter-add x8, other arithmetic, local(): total.at[:, right_cells]  235 us
    psum x5, blocking collectives, modal_total(): return lax.psum(local_part, 'cell')  156 us
    gather x32, local copies, waits for them, and re-layouts, local(): jnp.take(resid, source_rows[var], axis=0)  43.6 us
    dot_general x28, matrix products, wide_dot(): jnp.dot(left, right, precision=lax.Precision.HIGHEST, preferred_element_t...  36.4 us
  transfers between devices with their start and end apart: 8, of which 6 were waited for; matrix products, arithmetic and copies ran while one was open for 2% of the time, Pallas kernels for 0%

commit v1 on v0

v1 whole, which is shorter than its diff:
```python
import functools
import math

import jax
import jax.numpy as jnp
from jax import lax
from jax.experimental import pallas as pl
from jax.experimental.pallas import tpu as pltpu
from jax.sharding import PartitionSpec as P

ITERS = 4
FREQUENCY = 0.04
F32 = jnp.float32
BF16 = jnp.bfloat16
MODE_ROWS = 32


def spectral_matrix(count):
    index = jnp.arange(count)
    apart = index[:, None] - index[None, :]
    angle = math.pi * apart.astype(F32) / count
    parity = jnp.where(apart % 2 == 0, 1.0, -1.0).astype(F32)
    safe_sin = jnp.where(apart == 0, 1.0, jnp.sin(angle))
    return jnp.where(apart == 0, 0.0, 0.5 * parity * jnp.cos(angle) / safe_sin)


def split(value):
    high = value.astype(BF16)
    return high, (value - high.astype(F32)).astype(BF16)


def mm(left, right):
    return jnp.dot(left, right, preferred_element_type=F32)


def mm_nt(left, right):
    return lax.dot_general(left, right, (((1,), (1,)), ((), ())), preferred_element_type=F32)


def kernel(
    n,
    seed_ref,
    inv_ref,
    w_in_ref,
    shapes_ref,
    gain_ref,
    faces_ref,
    g_ref,
    col_ref,
    send_ref,
    out_ref,
    part_ref,
    w_ref,
    left_hot,
    m_high,
    m_low,
    mg_high,
    mg_low,
    p_ref,
    sel_ref,
    x_ref,
    z_ref,
    base_ref,
    ab_ref,
    q_all,
    ghost_out,
    ghost_in,
    q_send,
    q_recv,
    g_send,
    g_recv,
):
    count, nvar, owned = seed_ref.shape
    modes = shapes_ref.shape[0]
    rows = count * nvar
    halo = send_ref.shape[1]
    nfaces = g_ref.shape[1]
    me = lax.axis_index("cell")
    peers = [lax.rem(me + d, n) for d in range(n)]

    barrier = pltpu.get_barrier_semaphore()
    for d in range(1, n):
        pl.semaphore_signal(barrier, inc=1, device_id={"cell": peers[d]}, device_id_type=pl.DeviceIdType.MESH)

    left = faces_ref[0:1, :]
    right = faces_ref[1:2, :]
    g_high, g_low = split(g_ref[...])
    g_high = g_high.astype(F32)
    g_low = g_low.astype(F32)
    step = 128
    tall = owned + halo

    @pl.loop(0, tall // step)
    def _(t):
        at = pl.multiple_of(t * step, step)
        hit = left == lax.broadcasted_iota(jnp.int32, (step, nfaces), 0) + at
        left_hot[0, pl.ds(at, step), :] = jnp.where(hit, g_high, 0.0).astype(BF16)
        left_hot[1, pl.ds(at, step), :] = jnp.where(hit, g_low, 0.0).astype(BF16)

    wide = 256
    tall_step = tall // 3

    @pl.loop(0, owned // wide)
    def _(t):
        at = pl.multiple_of(t * wide, wide)
        hit = right == lax.broadcasted_iota(jnp.int32, (wide, nfaces), 0) + at
        hot = jnp.where(hit, 1.0, 0.0).astype(BF16)
        for part in range(3):
            r0 = part * tall_step
            block = mm_nt(left_hot[0, r0 : r0 + tall_step, :], hot) + mm_nt(left_hot[1, r0 : r0 + tall_step, :], hot)
            high, low = split(block)
            here = min(r0 + tall_step, owned) - r0
            m_high[r0 : r0 + here, pl.ds(at, wide)] = high[:here]
            m_low[r0 : r0 + here, pl.ds(at, wide)] = low[:here]
            if here < tall_step:
                mg_high[0:halo, pl.ds(at, wide)] = high[here:]
                mg_low[0:halo, pl.ds(at, wide)] = low[here:]

    hit = right == lax.broadcasted_iota(jnp.int32, (halo, nfaces), 0) + (owned + halo)
    upper_high = jnp.where(hit, g_high, 0.0).astype(BF16)
    upper_low = jnp.where(hit, g_low, 0.0).astype(BF16)
    upper_hot = jnp.concatenate([upper_high, upper_low], axis=0)

    @pl.loop(0, owned // wide)
    def _(t):
        at = pl.multiple_of(t * wide, wide)
        hit = left == lax.broadcasted_iota(jnp.int32, (wide, nfaces), 0) + at
        hot = jnp.where(hit, 1.0, 0.0).astype(BF16)
        block = mm_nt(upper_hot, hot)
        high, low = split(block[:halo] + block[halo:])
        mg_high[halo:, pl.ds(at, wide)] = high
        mg_low[halo:, pl.ds(at, wide)] = low

    w_high, w_low = split(w_in_ref[...])
    lane = lax.broadcasted_iota(jnp.int32, (3 * rows, 3 * rows), 1)
    w_ref[...] = jnp.where(lane < 2 * rows, w_high.astype(F32), w_low.astype(F32)).astype(BF16)
    send_row = jnp.concatenate([send_ref[0:1, :], send_ref[1:2, :]], axis=1)
    sel_ref[...] = jnp.where(
        send_row == lax.broadcasted_iota(jnp.int32, (owned, 2 * halo), 0), 1.0, 0.0
    ).astype(BF16)
    for v in range(nvar):
        shape_v = shapes_ref[:, v, :]
        shape_v = jnp.concatenate([shape_v, jnp.zeros((MODE_ROWS - modes, owned), F32)], axis=0)
        high, low = split(shape_v)
        p_ref[v, 0:MODE_ROWS, :] = high
        p_ref[v, MODE_ROWS:, :] = low
        z_ref[v * count : (v + 1) * count, :] = seed_ref[:, v, :]
    colours = col_ref[...]

    def update(colour):
        mask = colours == colour
        for w in range(nvar):
            spot = slice(w * count, (w + 1) * count)
            total = inv_ref[0, w].astype(F32) * z_ref[0:count, :]
            for v in range(1, nvar):
                total = total + inv_ref[v, w].astype(F32) * z_ref[v * count : (v + 1) * count, :]
            x_ref[spot, :] = jnp.where(mask, total, x_ref[spot, :])

    def coupling():
        high, low = split(x_ref[...])
        both = mm(w_ref[...], jnp.concatenate([high, low, high], axis=0))
        a_high, a_low = split(both[:rows])
        b_high, b_low = split(both[rows : 2 * rows])
        ab_ref[0, 0:rows, :] = a_high
        ab_ref[0, rows:, :] = a_low
        ab_ref[1, 0:rows, :] = b_high
        ab_ref[1, rows:, :] = b_low
        z_ref[...] = both[2 * rows :]

        @pl.loop(0, owned // wide)
        def _(t):
            at = pl.multiple_of(t * wide, wide)
            cols = pl.ds(at, wide)
            one = mm(ab_ref[0], m_high[:, cols]) + mm_nt(ab_ref[1], m_high[cols, :])
            two = mm(ab_ref[0, 0:rows, :], m_low[:, cols]) + mm_nt(ab_ref[1, 0:rows, :], m_low[cols, :])
            z_ref[:, cols] = z_ref[:, cols] + (one[:rows] + one[rows:] + two)

    def modal_copies(turn):
        return [
            pltpu.make_async_remote_copy(
                src_ref=q_all.at[turn, me],
                dst_ref=q_all.at[turn, me],
                send_sem=q_send.at[turn, d],
                recv_sem=q_recv.at[turn, d],
                device_id={"cell": peers[d]},
                device_id_type=pl.DeviceIdType.MESH,
            )
            for d in range(1, n)
        ]

    def ghost_copies(turn):
        return [
            pltpu.make_async_remote_copy(
                src_ref=ghost_out.at[turn, way],
                dst_ref=ghost_in.at[turn, 1 - way],
                send_sem=g_send.at[turn, way],
                recv_sem=g_recv.at[turn, way],
                device_id={"cell": peers[n - 1 if way == 0 else 1]},
                device_id_type=pl.DeviceIdType.MESH,
            )
            for way in range(2)
        ]

    def start_exchange(turn):
        high, low = split(x_ref[...])
        copies = []
        if turn < ITERS - 1:
            picked = mm(jnp.concatenate([high, low], axis=0), sel_ref[...])
            picked = picked[:rows] + picked[rows:]
            ghost_out[turn, 0] = picked[:, :halo]
            ghost_out[turn, 1] = picked[:, halo:]
            copies = ghost_copies(turn)
            if turn == 0:
                pl.semaphore_wait(barrier, n - 1)
            for copy in copies:
                copy.start()
        gram = jnp.zeros((2 * count, 2 * MODE_ROWS), F32)
        for v in range(nvar):
            spot = slice(v * count, (v + 1) * count)
            gram = gram + mm_nt(jnp.concatenate([high[spot], low[spot]], axis=0), p_ref[v])
        gram = gram[:count] + gram[count:]
        part = gram[:, :MODE_ROWS] + gram[:, MODE_ROWS:]
        q_all[turn, me] = jnp.concatenate([part, jnp.zeros((count, 128 - MODE_ROWS), F32)], axis=1)
        modal = modal_copies(turn)
        for copy in modal:
            copy.start()
        return copies + modal

    def modal_sum(turn):
        total = q_all[turn, 0]
        for d in range(1, n):
            total = total + q_all[turn, d]
        return total

    x_ref[...] = jnp.zeros((rows, owned), F32)
    update(0)
    coupling()
    for v in range(nvar):
        spot = slice(v * count, (v + 1) * count)
        z_ref[spot, :] = seed_ref[:, v, :] - z_ref[spot, :]
    update(1)
    copies = start_exchange(0)
    for sweep in range(1, ITERS):
        coupling()
        for copy in copies:
            copy.wait()
        low_part = ghost_in[sweep - 1, 0]
        up_part = ghost_in[sweep - 1, 1]
        high, low = split(jnp.concatenate([low_part, up_part], axis=1))
        both = mm(w_ref[0 : 2 * rows, :], jnp.concatenate([high, low, high], axis=0))
        ghost_ab = jnp.concatenate([both[:rows, :halo], both[rows:, halo:]], axis=1)
        high, low = split(ghost_ab)
        term = mm(jnp.concatenate([high, low], axis=0), mg_high[...])
        term = term[:rows] + term[rows:] + mm(high, mg_low[...])
        lam = modal_sum(sweep - 1)[:, :MODE_ROWS] * gain_ref[...]
        lam_high, lam_low = split(lam)
        lam_both = jnp.concatenate([lam_high, lam_low], axis=0)
        for v in range(nvar):
            spot = slice(v * count, (v + 1) * count)
            lift = mm(lam_both, p_ref[v, 0:MODE_ROWS, :])
            lift = lift[:count] + lift[count:] + mm(lam_high, p_ref[v, MODE_ROWS:, :])
            base = seed_ref[:, v, :] + lift - term[spot]
            base_ref[spot, :] = base
            z_ref[spot, :] = base - z_ref[spot, :]
        update(0)
        coupling()
        z_ref[...] = base_ref[...] - z_ref[...]
        update(1)
        copies = start_exchange(sweep)
    for v in range(nvar):
        out_ref[:, v, :] = x_ref[v * count : (v + 1) * count, :]
    for copy in copies:
        copy.wait()
    part_ref[...] = modal_sum(ITERS - 1)[:, :modes]


def local(
    adjoint_seed,
    inv_blocks,
    flux_jacobians,
    modal_shapes,
    modal_gain,
    face_cells,
    face_weights,
    colours,
    send_cells,
):
    n = lax.axis_size("cell")
    count, nvar, owned = adjoint_seed.shape
    modes = modal_shapes.shape[0]
    rows = count * nvar
    halo = send_cells.shape[1]
    nfaces = face_weights.shape[0]
    eye_inst = jnp.eye(count, dtype=F32)
    eye_var = jnp.eye(nvar, dtype=F32)
    left_matrix = (
        jnp.transpose(flux_jacobians[0], (2, 0, 1))[:, :, :, None] * eye_inst[None, :, None, :]
    ).reshape(rows, rows)
    right_matrix = (
        jnp.transpose(flux_jacobians[1], (2, 0, 1))[:, :, :, None] * eye_inst[None, :, None, :]
    ).reshape(rows, rows)
    spectral = FREQUENCY * spectral_matrix(count)
    spectral_rows = (eye_var[:, None, :, None] * spectral.T[None, :, None, :]).reshape(rows, rows)
    stacked = jnp.concatenate([left_matrix, right_matrix, spectral_rows], axis=0)
    weights = jnp.concatenate([stacked, stacked, stacked], axis=1)
    inverse = jnp.transpose(inv_blocks, (1, 2, 0, 3))
    gain = jnp.concatenate([modal_gain, jnp.zeros((MODE_ROWS - modes,), F32)])[None, :]
    vmem = pl.BlockSpec(memory_space=pltpu.VMEM)
    tall = owned + halo
    turns = ITERS
    out, part = pl.pallas_call(
        functools.partial(kernel, n),
        out_shape=(
            jax.ShapeDtypeStruct((count, nvar, owned), F32),
            jax.ShapeDtypeStruct((count, modes), F32),
        ),
        in_specs=[vmem] * 9,
        out_specs=(vmem, vmem),
        scratch_shapes=[
            pltpu.VMEM((3 * rows, 3 * rows), BF16),
            pltpu.VMEM((2, tall, nfaces), BF16),
            pltpu.VMEM((owned, owned), BF16),
            pltpu.VMEM((owned, owned), BF16),
            pltpu.VMEM((2 * halo, owned), BF16),
            pltpu.VMEM((2 * halo, owned), BF16),
            pltpu.VMEM((nvar, 2 * MODE_ROWS, owned), BF16),
            pltpu.VMEM((owned, 2 * halo), BF16),
            pltpu.VMEM((rows, owned), F32),
            pltpu.VMEM((rows, owned), F32),
            pltpu.VMEM((rows, owned), F32),
            pltpu.VMEM((2, 2 * rows, owned), BF16),
            pltpu.VMEM((turns, n, count, 128), F32),
            pltpu.VMEM((turns - 1, 2, rows, halo), F32),
            pltpu.VMEM((turns - 1, 2, rows, halo), F32),
            pltpu.SemaphoreType.DMA((turns, n)),
            pltpu.SemaphoreType.DMA((turns, n)),
            pltpu.SemaphoreType.DMA((turns - 1, 2)),
            pltpu.SemaphoreType.DMA((turns - 1, 2)),
        ],
        compiler_params=pltpu.CompilerParams(
            collective_id=0, has_side_effects=True, vmem_limit_bytes=56 * 1024 * 1024
        ),
    )(
        adjoint_seed,
        inverse,
        weights,
        modal_shapes,
        gain,
        face_cells,
        face_weights[None, :],
        colours[None, :],
        send_cells,
    )
    return out, part


def solution(mesh):
    return jax.shard_map(
        local,
        mesh=mesh,
        in_specs=(
            P("group", None, "cell"),
            P("group", None, None, "cell"),
            P(None, "group", None, None),
            P(None, None, "cell"),
            P("group"),
            P(None, "cell"),
            P("cell"),
            P("cell"),
            P(None, "cell"),
        ),
        out_specs=(P("group", None, "cell"), P("group", None)),
        check_vma=False,
    )
```

time: 833 us -> 74.2 us (0.09); the launches traced: 821 us -> 73.9 us
  other arithmetic: 498 us -> 1.26 us
  blocking collectives: 156 us -> 0 us
  local copies, waits for them, and re-layouts: 96.2 us -> 7.17 us
  Pallas kernels: 0 us -> 64.8 us
  matrix products: 47.3 us -> 0 us
  waiting for transfers between devices: 14.2 us -> 0 us
    scatter-add x16 -> x0, other arithmetic: 477 us -> none  [the longest x8 242 us: local(): total.at[:, left_cells]]
    psum x5 -> x0, blocking collectives: 156 us -> none  [modal_total(): return lax.psum(local_part, 'cell')]
    gather x61 -> x0, local copies, waits for them, and re-layouts: 64.8 us -> none  [the longest x32 43.6 us: local(): jnp.take(resid, source_rows[var], axis=0)]
    pallas_call x0 -> x1, Pallas kernels: none -> 64.8 us  [local(): pl.pallas_call(functools.partial(kernel, n), out_shape=(jax.ShapeDtypeStr...]
    dot_general x33 -> x0, matrix products: 47.3 us -> none  [the longest x28 36.4 us: wide_dot(): jnp.dot(left, right, precision=lax.Precision.HIGHEST, preferred_element_t...]
    select_n x18 -> x0, other arithmetic: 15.6 us -> none  [the longest x8 11.8 us: local(): state = jnp.where(colour_mask == colour, updated, state)]
    ppermute x8 -> x0, waiting for transfers between devices: 14.2 us -> none  [from_behind(): lax.ppermute(value, axis, [(i, (i + by) % devices) for i in range(devices)])]
    unnamed x118 -> x11, local copies, waits for them, and re-layouts: 13.2 us -> 3.48 us
  transfers between devices with their start and end apart: 8 -> 0, of which waited for: 6 -> 0; matrix products, arithmetic and copies ran while one was open for 2% -> 0% of each run, Pallas kernels for 0% -> 0%
where the time goes in v1:
time: 74.2 us; the launch traced here: 73.9 us
  Pallas kernels  64.8 us (87%)
  local copies, waits for them, and re-layouts  7.17 us (10%)
  other arithmetic  1.26 us (2%)
    pallas_call x1, Pallas kernels, local(): pl.pallas_call(functools.partial(kernel, n), out_shape=(jax.ShapeDtypeStr...  64.8 us
    unnamed x11, local copies, waits for them, and re-layouts  3.48 us
    pallas_call x1, local copies, waits for them, and re-layouts, local(): pl.pallas_call(functools.partial(kernel, n), out_shape=(jax.ShapeDtypeStr...  1.96 us

profile of v1, /device:TPU:0, one launch (start us, length us, event | category | flops | bytes accessed | tf_op | source)
XLA Modules:
  0.0 73.9 jit_solution(1143325991218667611)
XLA Ops:
  0.6 0.0 copy-start.2
  0.6 1.2 %pad_bitcast_fusion.gain_ref = f32[1,32]{1,0:T(1,128)} fusion(f32[20]{0:T(128)} %param.13), kind=kLoop, calls=%fused_computation.19 | loop fusion | bytes 208 | tf_op jit(solution)/shard_map/broadcast_in_dim | solution.py:307
  1.8 0.1 select_multiply_fusion
  1.9 0.0 copy-done.2
  1.9 0.1 copy.25
  2.0 0.1 copy.26
  2.1 0.0 copy-start.1
  2.1 0.1 broadcast_multiply_fusion
  2.2 0.1 mul.98
  2.4 0.8 %copy-done.1 = f32[16,5,1024]{2,0,1:T(8,128)S(1)} copy-done((f32[16,5,1024]{2,0,1:T(8,128)S(1)}, f32[16,5,1024]{2,0,1:T(8,128)}, u32[]{:S(2)}) %copy-start.1) | copy-done | bytes 327704
  3.1 1.0 %copy.20.seed_ref = f32[16,5,1024]{2,1,0:T(8,128)} copy(f32[16,5,1024]{2,0,1:T(8,128)S(1)} %copy-done.1) | data formatting | bytes 655360 | tf_op args[0]
  4.1 0.2 broadcast_multiply_fusion.2
  4.4 0.0 copy-start
  4.4 0.1 mul.86
  4.5 0.1 mul.89
  4.6 0.9 %maximum_maximum_fusion.w_in_ref = f32[240,240]{1,0:T(8,128)} fusion(f32[80,80]{1,0:T(8,128)S(1)} %mul.98, f32[80,80]{1,0:T(8,128)S(1)} %mul.89, f32[80,80]{1,0:T(8,128)S(1)} %mul.86), kind=kLoop, calls=%fused_computation | loop fusion | flops 460800 | bytes 307200 | tf_op jit(solution)/shard_map/concatenate | solution.py:305
  5.5 0.0 copy-done
  5.5 1.1 %copy.21.shapes_ref = f32[20,5,1024]{2,1,0:T(8,128)} copy(f32[20,5,1024]{2,0,1:T(8,128)S(1)} %copy-done) | data formatting | bytes 819200 | tf_op args[3]
  6.6 64.8 %shard_map.104 = (f32[16,5,1024]{2,1,0:T(8,128)}, f32[16,20]{1,0:T(8,128)}) custom-call(f32[16,5,1024]{2,1,0:T(8,128)} %copy.20.seed_ref, bf16[5,5,16,1024]{3,2,1,0:T(8,128)(2,1)} %bitcast.13, f32[240,240]{1,0:T(8,128)} %maximum_maximum_fusion.w_in_ref, f32[20,5,1024]{2,1,0:T(8,128)} %copy.21.shapes_ref, f32[1,32]{1,0:T(1,128)} %pad_bitcast_fusion.gain_ref, ...), custom_call_target="tpu_custom_call" | custom-call | tf_op jit(solution)/shard_map/pallas_call | solution.py:311
  71.3 0.0 copy-start.3
  71.3 2.0 %copy.22 = f32[16,5,1024]{2,0,1:T(8,128)} copy(f32[16,5,1024]{2,1,0:T(8,128)} %get-tuple-element.4) | data formatting | bytes 655360 | tf_op jit(solution)/shard_map/pallas_call | solution.py:311
  73.3 0.0 copy-done.3
  73.3 0.6 copy.28
  (3 shorter events, 0.0 us)
Async XLA Ops:
  0.6 1.3 %copy-start.2 = (f32[2,16,5,5]{1,0,3,2:T(2,128)S(1)}, f32[2,16,5,5]{1,0,3,2:T(2,128)}, u32[]{:S(2)}) copy-start(f32[2,16,5,5]{1,0,3,2:T(2,128)} %param.11) | copy-start | bytes 9604
  2.1 1.0 %copy-start.1 = (f32[16,5,1024]{2,0,1:T(8,128)S(1)}, f32[16,5,1024]{2,0,1:T(8,128)}, u32[]{:S(2)}) copy-start(f32[16,5,1024]{2,0,1:T(8,128)} %param.9) | copy-start | bytes 983044
  4.4 1.1 %copy-start = (f32[20,5,1024]{2,0,1:T(8,128)S(1)}, f32[20,5,1024]{2,0,1:T(8,128)}, u32[]{:S(2)}) copy-start(f32[20,5,1024]{2,0,1:T(8,128)} %param.12) | copy-start | bytes 1228804
  71.3 2.0 %copy-start.3 = (f32[16,20]{1,0:T(8,128)S(1)}, f32[16,20]{1,0:T(8,128)}, u32[]{:S(2)}) copy-start(f32[16,20]{1,0:T(8,128)} %get-tuple-element.13) | copy-start | bytes 3844

commit v2 on v1

--- a/solution.py
+++ b/solution.py
@@ -51,6 +51,7 @@
     out_ref,
     part_ref,
     w_ref,
+    gain_pad,
     left_hot,
     m_high,
     m_low,
@@ -70,8 +71,8 @@
     g_send,
     g_recv,
 ):
-    count, nvar, owned = seed_ref.shape
-    modes = shapes_ref.shape[0]
+    nvar, count, owned = seed_ref.shape
+    modes = shapes_ref.shape[1]
     rows = count * nvar
     halo = send_ref.shape[1]
     nfaces = g_ref.shape[1]
@@ -85,17 +86,22 @@
     left = faces_ref[0:1, :]
     right = faces_ref[1:2, :]
     g_high, g_low = split(g_ref[...])
-    g_high = g_high.astype(F32)
-    g_low = g_low.astype(F32)
+    one = jnp.ones((1, nfaces), BF16)
     step = 128
     tall = owned + halo
+
+    def hot(index, start, size, value):
+        lines = lax.broadcasted_iota(jnp.int32, (size, 128), 0).astype(jnp.int16)
+        lines = jnp.concatenate([lines] * (nfaces // 128), axis=1)
+        near = jnp.broadcast_to((index - start).astype(jnp.int16), (size, nfaces))
+        zero = jnp.zeros((size, nfaces), BF16)
+        return jnp.where(near == lines, jnp.broadcast_to(value, (size, nfaces)), zero)
 
     @pl.loop(0, tall // step)
     def _(t):
         at = pl.multiple_of(t * step, step)
-        hit = left == lax.broadcasted_iota(jnp.int32, (step, nfaces), 0) + at
-        left_hot[0, pl.ds(at, step), :] = jnp.where(hit, g_high, 0.0).astype(BF16)
-        left_hot[1, pl.ds(at, step), :] = jnp.where(hit, g_low, 0.0).astype(BF16)
+        left_hot[0, pl.ds(at, step), :] = hot(left, at, step, g_high)
+        left_hot[1, pl.ds(at, step), :] = hot(left, at, step, g_low)
 
     wide = 256
     tall_step = tall // 3
@@ -103,11 +109,10 @@
     @pl.loop(0, owned // wide)
     def _(t):
         at = pl.multiple_of(t * wide, wide)
-        hit = right == lax.broadcasted_iota(jnp.int32, (wide, nfaces), 0) + at
-        hot = jnp.where(hit, 1.0, 0.0).astype(BF16)
+        right_hot = hot(right, at, wide, one)
         for part in range(3):
             r0 = part * tall_step
-            block = mm_nt(left_hot[0, r0 : r0 + tall_step, :], hot) + mm_nt(left_hot[1, r0 : r0 + tall_step, :], hot)
+            block = mm_nt(left_hot[0, r0 : r0 + tall_step, :], right_hot) + mm_nt(left_hot[1, r0 : r0 + tall_step, :], right_hot)
             high, low = split(block)
             here = min(r0 + tall_step, owned) - r0
             m_high[r0 : r0 + here, pl.ds(at, wide)] = high[:here]
@@ -116,35 +121,37 @@
                 mg_high[0:halo, pl.ds(at, wide)] = high[here:]
                 mg_low[0:halo, pl.ds(at, wide)] = low[here:]
 
-    hit = right == lax.broadcasted_iota(jnp.int32, (halo, nfaces), 0) + (owned + halo)
-    upper_high = jnp.where(hit, g_high, 0.0).astype(BF16)
-    upper_low = jnp.where(hit, g_low, 0.0).astype(BF16)
+    upper_high = hot(right, owned + halo, halo, g_high)
+    upper_low = hot(right, owned + halo, halo, g_low)
     upper_hot = jnp.concatenate([upper_high, upper_low], axis=0)
 
     @pl.loop(0, owned // wide)
     def _(t):
         at = pl.multiple_of(t * wide, wide)
-        hit = left == lax.broadcasted_iota(jnp.int32, (wide, nfaces), 0) + at
-        hot = jnp.where(hit, 1.0, 0.0).astype(BF16)
-        block = mm_nt(upper_hot, hot)
+        block = mm_nt(upper_hot, hot(left, at, wide, one))
         high, low = split(block[:halo] + block[halo:])
         mg_high[halo:, pl.ds(at, wide)] = high
         mg_low[halo:, pl.ds(at, wide)] = low
 
     w_high, w_low = split(w_in_ref[...])
-    lane = lax.broadcasted_iota(jnp.int32, (3 * rows, 3 * rows), 1)
-    w_ref[...] = jnp.where(lane < 2 * rows, w_high.astype(F32), w_low.astype(F32)).astype(BF16)
+    lane = lax.broadcasted_iota(jnp.int32, (rows, 3 * rows), 1)
+    line = lax.broadcasted_iota(jnp.int32, (rows, 3 * rows), 0)
+    first = jnp.where((lane == line) | (lane == line + rows), 1.0, 0.0).astype(BF16)
+    last = jnp.where(lane == line + 2 * rows, 1.0, 0.0).astype(BF16)
+    w_ref[...] = (mm(w_high, first) + mm(w_low, last)).astype(BF16)
+    gain_pad[...] = jnp.zeros((1, 128), F32)
+    gain_pad[:, 0:modes] = gain_ref[...]
     send_row = jnp.concatenate([send_ref[0:1, :], send_ref[1:2, :]], axis=1)
     sel_ref[...] = jnp.where(
         send_row == lax.broadcasted_iota(jnp.int32, (owned, 2 * halo), 0), 1.0, 0.0
     ).astype(BF16)
     for v in range(nvar):
-        shape_v = shapes_ref[:, v, :]
+        shape_v = shapes_ref[v]
         shape_v = jnp.concatenate([shape_v, jnp.zeros((MODE_ROWS - modes, owned), F32)], axis=0)
         high, low = split(shape_v)
         p_ref[v, 0:MODE_ROWS, :] = high
         p_ref[v, MODE_ROWS:, :] = low
-        z_ref[v * count : (v + 1) * count, :] = seed_ref[:, v, :]
+        z_ref[v * count : (v + 1) * count, :] = seed_ref[v]
     colours = col_ref[...]
 
     def update(colour):
@@ -237,7 +244,7 @@
     coupling()
     for v in range(nvar):
         spot = slice(v * count, (v + 1) * count)
-        z_ref[spot, :] = seed_ref[:, v, :] - z_ref[spot, :]
+        z_ref[spot, :] = seed_ref[v] - z_ref[spot, :]
     update(1)
     copies = start_exchange(0)
     for sweep in range(1, ITERS):
@@ -252,14 +259,14 @@
         high, low = split(ghost_ab)
         term = mm(jnp.concatenate([high, low], axis=0), mg_high[...])
         term = term[:rows] + term[rows:] + mm(high, mg_low[...])
-        lam = modal_sum(sweep - 1)[:, :MODE_ROWS] * gain_ref[...]
+        lam = modal_sum(sweep - 1)[:, :MODE_ROWS] * gain_pad[:, :MODE_ROWS]
         lam_high, lam_low = split(lam)
         lam_both = jnp.concatenate([lam_high, lam_low], axis=0)
         for v in range(nvar):
             spot = slice(v * count, (v + 1) * count)
             lift = mm(lam_both, p_ref[v, 0:MODE_ROWS, :])
             lift = lift[:count] + lift[count:] + mm(lam_high, p_ref[v, MODE_ROWS:, :])
-            base = seed_ref[:, v, :] + lift - term[spot]
+            base = seed_ref[v] + lift - term[spot]
             base_ref[spot, :] = base
             z_ref[spot, :] = base - z_ref[spot, :]
         update(0)
@@ -268,7 +275,7 @@
         update(1)
         copies = start_exchange(sweep)
     for v in range(nvar):
-        out_ref[:, v, :] = x_ref[v * count : (v + 1) * count, :]
+        out_ref[v] = x_ref[v * count : (v + 1) * count, :]
     for copy in copies:
         copy.wait()
     part_ref[...] = modal_sum(ITERS - 1)[:, :modes]
@@ -302,22 +309,21 @@
     spectral = FREQUENCY * spectral_matrix(count)
     spectral_rows = (eye_var[:, None, :, None] * spectral.T[None, :, None, :]).reshape(rows, rows)
     stacked = jnp.concatenate([left_matrix, right_matrix, spectral_rows], axis=0)
-    weights = jnp.concatenate([stacked, stacked, stacked], axis=1)
     inverse = jnp.transpose(inv_blocks, (1, 2, 0, 3))
-    gain = jnp.concatenate([modal_gain, jnp.zeros((MODE_ROWS - modes,), F32)])[None, :]
     vmem = pl.BlockSpec(memory_space=pltpu.VMEM)
     tall = owned + halo
     turns = ITERS
     out, part = pl.pallas_call(
         functools.partial(kernel, n),
         out_shape=(
-            jax.ShapeDtypeStruct((count, nvar, owned), F32),
+            jax.ShapeDtypeStruct((nvar, count, owned), F32),
             jax.ShapeDtypeStruct((count, modes), F32),
         ),
         in_specs=[vmem] * 9,
         out_specs=(vmem, vmem),
         scratch_shapes=[
             pltpu.VMEM((3 * rows, 3 * rows), BF16),
+            pltpu.VMEM((1, 128), F32),
             pltpu.VMEM((2, tall, nfaces), BF16),
             pltpu.VMEM((owned, owned), BF16),
             pltpu.VMEM((owned, owned), BF16),
@@ -341,17 +347,17 @@
             collective_id=0, has_side_effects=True, vmem_limit_bytes=56 * 1024 * 1024
         ),
     )(
-        adjoint_seed,
+        jnp.transpose(adjoint_seed, (1, 0, 2)),
         inverse,
-        weights,
-        modal_shapes,
-        gain,
+        stacked,
+        jnp.transpose(modal_shapes, (1, 0, 2)),
+        modal_gain[None, :],
         face_cells,
         face_weights[None, :],
         colours[None, :],
         send_cells,
     )
-    return out, part
+    return jnp.transpose(out, (1, 0, 2)), part
 
 
 def solution(mesh):

time: 74.2 us -> 68.8 us (0.927)
  local copies, waits for them, and re-layouts: 7.17 us -> 3.71 us
  Pallas kernels: 64.8 us -> 63.2 us
    pallas_call x1 -> x0, local copies, waits for them, and re-layouts: 1.96 us -> none  [local(): pl.pallas_call(functools.partial(kernel, n), out_shape=(jax.ShapeDtypeStr...]
    pallas_call x1, Pallas kernels: 64.8 us -> 63.2 us  [local(): pl.pallas_call(functools.partial(kernel, n), out_shape=(jax.ShapeDtypeStr...]
    broadcast_in_dim x1 -> x0, local copies, waits for them, and re-layouts: 1.17 us -> none  [local(): jnp.concatenate([modal_gain, jnp.zeros((MODE_ROWS - modes,), F32)])[None, :]]
    unnamed x11 -> x4, local copies, waits for them, and re-layouts: 3.48 us -> 2.33 us
    slice x1, local copies, waits for them, and re-layouts: 0.02 us -> 0.84 us  [local(): flux_jacobians[0]]
where the time goes in v2:
time: 68.8 us; the launch traced here: 68.6 us
  Pallas kernels  63.2 us (92%)
  local copies, waits for them, and re-layouts  3.71 us (5%)
  other arithmetic  1.05 us (2%)
  between operations  0.7 us (1%)
    pallas_call x1, Pallas kernels, local(): pl.pallas_call(functools.partial(kernel, n), out_shape=(jax.ShapeDtypeStr...  63.2 us
    unnamed x4, local copies, waits for them, and re-layouts  2.33 us

profile of v2, /device:TPU:0, one launch (start us, length us, event | category | flops | bytes accessed | tf_op | source)
XLA Modules:
  0.0 68.6 jit_solution(15150398026554251127)
XLA Ops:
  0.6 0.8 %fusion.8 = (f32[1,16,5,5]{1,0,3,2:T(1,128)S(1)}, f32[1,16,5,5]{1,0,3,2:T(1,128)S(1)}) fusion(f32[2,16,5,5]{1,0,3,2:T(2,128)} %param.11), kind=kLoop, calls=%fused_computation.19 | loop fusion | bytes 6400 | tf_op jit(solution)/shard_map/slice | solution.py:304
  1.5 0.1 copy.19
  1.6 0.1 copy.20
  1.7 0.2 broadcast_multiply_fusion.2
  1.9 0.1 mul.86
  2.0 0.1 mul.89
  2.2 0.1 select_multiply_fusion
  2.2 0.1 broadcast_multiply_fusion
  2.3 0.1 mul.98
  2.5 0.7 pad_maximum_fusion.w_in_ref
  3.1 63.2 %shard_map.104 = (f32[5,16,1024]{2,1,0:T(8,128)}, f32[16,20]{1,0:T(8,128)}) custom-call(f32[5,16,1024]{2,1,0:T(8,128)} %bitcast.18, bf16[5,5,16,1024]{3,2,1,0:T(8,128)(2,1)} %bitcast.15, f32[240,80]{1,0:T(8,128)} %pad_maximum_fusion.w_in_ref, f32[5,20,1024]{2,1,0:T(8,128)} %bitcast.16, f32[1,20]{1,0:T(1,128)} %bitcast.23, s32[2,3072]{1,0:T(2,128)} %faces_ref.1, ...), custom_call_target="tpu_custom_call" | custom-call | tf_op jit(solution)/shard_map/pallas_call | solution.py:316
  66.3 0.0 copy-start
  66.3 1.7 %copy.23 = f32[16,5,1024]{2,0,1:T(8,128)} copy(f32[16,5,1024]{2,0,1:T(8,128)} %bitcast.17) | data formatting | bytes 655360
  68.0 0.0 copy-done
  68.0 0.6 copy.24
  (2 shorter events, 0.0 us)
Async XLA Ops:
  66.3 1.7 %copy-start = (f32[16,20]{1,0:T(8,128)S(1)}, f32[16,20]{1,0:T(8,128)}, u32[]{:S(2)}) copy-start(f32[16,20]{1,0:T(8,128)} %get-tuple-element.13) | copy-start | bytes 3844

commit v3 on v2

--- a/solution.py
+++ b/solution.py
@@ -12,6 +12,8 @@
 FREQUENCY = 0.04
 F32 = jnp.float32
 BF16 = jnp.bfloat16
+F8 = jnp.float8_e4m3fn
+LIFT = 256.0
 MODE_ROWS = 32
 
 
@@ -53,6 +55,7 @@
     w_ref,
     gain_pad,
     left_hot,
+    left_low,
     m_high,
     m_low,
     mg_high,
@@ -100,8 +103,8 @@
     @pl.loop(0, tall // step)
     def _(t):
         at = pl.multiple_of(t * step, step)
-        left_hot[0, pl.ds(at, step), :] = hot(left, at, step, g_high)
-        left_hot[1, pl.ds(at, step), :] = hot(left, at, step, g_low)
+        left_hot[pl.ds(at, step), :] = hot(left, at, step, g_high)
+        left_low[pl.ds(at, step), :] = (hot(left, at, step, g_low).astype(F32) * LIFT).astype(F8)
 
     wide = 256
     tall_step = tall // 3
@@ -110,9 +113,11 @@
     def _(t):
         at = pl.multiple_of(t * wide, wide)
         right_hot = hot(right, at, wide, one)
+        right_low = right_hot.astype(F32).astype(F8)
         for part in range(3):
             r0 = part * tall_step
-            block = mm_nt(left_hot[0, r0 : r0 + tall_step, :], right_hot) + mm_nt(left_hot[1, r0 : r0 + tall_step, :], right_hot)
+            block = mm_nt(left_hot[r0 : r0 + tall_step, :], right_hot)
+            block = block + mm_nt(left_low[r0 : r0 + tall_step, :], right_low) * (1.0 / LIFT)
             high, low = split(block)
             here = min(r0 + tall_step, owned) - r0
             m_high[r0 : r0 + here, pl.ds(at, wide)] = high[:here]
@@ -227,7 +232,10 @@
             gram = gram + mm_nt(jnp.concatenate([high[spot], low[spot]], axis=0), p_ref[v])
         gram = gram[:count] + gram[count:]
         part = gram[:, :MODE_ROWS] + gram[:, MODE_ROWS:]
-        q_all[turn, me] = jnp.concatenate([part, jnp.zeros((count, 128 - MODE_ROWS), F32)], axis=1)
+        half = count // 2
+        q_all[turn, me] = jnp.concatenate(
+            [part[:half], part[half:], jnp.zeros((half, 128 - 2 * MODE_ROWS), F32)], axis=1
+        )
         modal = modal_copies(turn)
         for copy in modal:
             copy.start()
@@ -237,7 +245,7 @@
         total = q_all[turn, 0]
         for d in range(1, n):
             total = total + q_all[turn, d]
-        return total
+        return jnp.concatenate([total[:, :MODE_ROWS], total[:, MODE_ROWS : 2 * MODE_ROWS]], axis=0)
 
     x_ref[...] = jnp.zeros((rows, owned), F32)
     update(0)
@@ -324,7 +332,8 @@
         scratch_shapes=[
             pltpu.VMEM((3 * rows, 3 * rows), BF16),
             pltpu.VMEM((1, 128), F32),
-            pltpu.VMEM((2, tall, nfaces), BF16),
+            pltpu.VMEM((tall, nfaces), BF16),
+            pltpu.VMEM((tall, nfaces), F8),
             pltpu.VMEM((owned, owned), BF16),
             pltpu.VMEM((owned, owned), BF16),
             pltpu.VMEM((2 * halo, owned), BF16),
@@ -335,7 +344,7 @@
             pltpu.VMEM((rows, owned), F32),
             pltpu.VMEM((rows, owned), F32),
             pltpu.VMEM((2, 2 * rows, owned), BF16),
-            pltpu.VMEM((turns, n, count, 128), F32),
+            pltpu.VMEM((turns, n, count // 2, 128), F32),
             pltpu.VMEM((turns - 1, 2, rows, halo), F32),
             pltpu.VMEM((turns - 1, 2, rows, halo), F32),
             pltpu.SemaphoreType.DMA((turns, n)),

time: 68.8 us -> 63.4 us (0.922)
  Pallas kernels: 63.2 us -> 57.7 us
    pallas_call x1, Pallas kernels: 63.2 us -> 57.7 us  [local(): pl.pallas_call(functools.partial(kernel, n), out_shape=(jax.ShapeDtypeStr...]
where the time goes in v3:
time: 63.4 us; the launch traced here: 63.2 us
  Pallas kernels  57.7 us (91%)
  local copies, waits for them, and re-layouts  3.71 us (6%)
  other arithmetic  1.05 us (2%)
  between operations  0.7 us (1%)
    pallas_call x1, Pallas kernels, local(): pl.pallas_call(functools.partial(kernel, n), out_shape=(jax.ShapeDtypeStr...  57.7 us
    unnamed x4, local copies, waits for them, and re-layouts  2.33 us

profile of v3, /device:TPU:0, one launch (start us, length us, event | category | flops | bytes accessed | tf_op | source)
XLA Modules:
  0.0 63.2 jit_solution(719075737222886705)
XLA Ops:
  0.6 0.8 %fusion.8 = (f32[1,16,5,5]{1,0,3,2:T(1,128)S(1)}, f32[1,16,5,5]{1,0,3,2:T(1,128)S(1)}) fusion(f32[2,16,5,5]{1,0,3,2:T(2,128)} %param.11), kind=kLoop, calls=%fused_computation.19 | loop fusion | bytes 6400 | tf_op jit(solution)/shard_map/slice | solution.py:312
  1.5 0.1 copy.19
  1.6 0.1 copy.20
  1.7 0.2 broadcast_multiply_fusion.2
  1.9 0.1 mul.86
  2.0 0.1 mul.89
  2.2 0.1 select_multiply_fusion
  2.2 0.1 broadcast_multiply_fusion
  2.3 0.1 mul.98
  2.5 0.7 %pad_maximum_fusion.w_in_ref = f32[240,80]{1,0:T(8,128)} fusion(f32[80,80]{1,0:T(8,128)S(1)} %mul.98, f32[80,80]{1,0:T(8,128)S(1)} %mul.89, f32[80,80]{1,0:T(8,128)S(1)} %mul.86), kind=kLoop, calls=%fused_computation.3 | loop fusion | flops 38400 | bytes 153600 | tf_op jit(solution)/shard_map/concatenate | solution.py:319
  3.1 57.7 %shard_map.104 = (f32[5,16,1024]{2,1,0:T(8,128)}, f32[16,20]{1,0:T(8,128)}) custom-call(f32[5,16,1024]{2,1,0:T(8,128)} %bitcast.18, bf16[5,5,16,1024]{3,2,1,0:T(8,128)(2,1)} %bitcast.15, f32[240,80]{1,0:T(8,128)} %pad_maximum_fusion.w_in_ref, f32[5,20,1024]{2,1,0:T(8,128)} %bitcast.16, f32[1,20]{1,0:T(1,128)} %bitcast.23, s32[2,3072]{1,0:T(2,128)} %faces_ref.1, ...), custom_call_target="tpu_custom_call" | custom-call | tf_op jit(solution)/shard_map/pallas_call | solution.py:324
  60.8 0.0 copy-start
  60.8 1.7 %copy.23 = f32[16,5,1024]{2,0,1:T(8,128)} copy(f32[16,5,1024]{2,0,1:T(8,128)} %bitcast.17) | data formatting | bytes 655360
  62.6 0.0 copy-done
  62.6 0.6 copy.24
  (2 shorter events, 0.0 us)
Async XLA Ops:
  60.8 1.7 %copy-start = (f32[16,20]{1,0:T(8,128)S(1)}, f32[16,20]{1,0:T(8,128)}, u32[]{:S(2)}) copy-start(f32[16,20]{1,0:T(8,128)} %get-tuple-element.13) | copy-start | bytes 3844
